TPU v7x, 32 devices: a whole 2x2x4 slice. The times are simulated.
32 devices in a mesh: grid: 4 (over x, core), proc: 8 (over z, y).
Axes of the slice: x: 2, y: 2, z: 4, core: 2. Of those that a mesh axis runs over, the one named last changes fastest.
Arguments:
- rhs: float32 [3, 4, 8, 256, 1024], P(None, 'grid', 'proc'), may hold values from -6 to 6
- tile_pairs: int32 [2, 4, 8, 16], P(None, 'grid', 'proc'), may hold values from -1 to 15, as said below
- tiles: bfloat16 [2, 4, 8, 16, 256, 256], P(None, 'grid', 'proc'), may hold values from -0.125 to 0.125
- dinv: float32 [3, 4, 8, 256, 256], P(None, 'grid', 'proc'), as said below
Outputs:
- solution: float32 [3, 4, 8, 256, 1024], P(None, 'grid', 'proc')
Inputs may be any that keep to these rules, and one draw needn't show every extreme that they name: tile_pairs[t, g, p] holds distinct pair numbers in its first slots and -1 in the others; pair number q names block column q mod 8 and destination q // 8 (0: the same grid, 1: the partner grid). In every transition and grid one device uses all 16 slots and the others use 2 to 8 of them. Each dinv tile is lower triangular with diagonal entries between 0.5 and 1.4.
All inputs are finite; a program needn't handle non-finite values.
Results may differ from a plain program's by a relative error of at most 0.0021.
Values may be sent and summed in bfloat16 or wider, within the bound.
A program may use at most 128 MiB of HBM per device.

v0:
```python
import jax
import jax.numpy as jnp
from jax import lax
from jax.sharding import PartitionSpec as P


def from_partner(block, axis, apart):
    count = lax.axis_size(axis)
    route = []
    for low in range(count):
        high = low | 1 << apart
        if high != low and high < count:
            route += [(low, high), (high, low)]
    return lax.ppermute(block, axis, route)


def build_table(pairs, tile_set):
    slot_count = tile_set.shape[0]
    labels = lax.broadcasted_iota(jnp.int32, (slot_count, slot_count), 1)
    onehot = (pairs[:, None] == labels).astype(jnp.bfloat16)
    dense = jnp.einsum("sq,sij->qij", onehot, tile_set, preferred_element_type=jnp.float32)
    return dense.astype(jnp.bfloat16).reshape(
        2, slot_count // 2, tile_set.shape[1], tile_set.shape[2]
    )


def diagonal_solve(factor, values):
    return jnp.dot(
        factor, values, precision=lax.Precision.HIGHEST, preferred_element_type=jnp.float32
    )


def solve_levels(rhs_block, dinv_block, tables):
    levels = rhs_block.shape[0]
    current = diagonal_solve(dinv_block[0], rhs_block[0])
    solved = [current]
    for height in range(1, levels):
        dense_table = tables[height - 1]
        outgoing = current.astype(jnp.bfloat16)[None]
        partial_value = jnp.einsum(
            "dkij,kjr->dir",
            dense_table,
            lax.all_gather(outgoing, "proc", axis=0, tiled=True),
            preferred_element_type=jnp.float32,
        )
        partner = from_partner(partial_value[1], "grid", height - 1)
        update = partial_value[0] + partner
        current = diagonal_solve(dinv_block[height], rhs_block[height] - update)
        solved.append(current)
    return jnp.stack(solved)


def body(rhs, tile_pairs, tiles, dinv):
    rhs_block = rhs[:, 0, 0]
    dinv_block = dinv[:, 0, 0]
    tables = [
        build_table(tile_pairs[number, 0, 0], tiles[number, 0, 0])
        for number in range(tile_pairs.shape[0])
    ]
    solved = solve_levels(rhs_block, dinv_block, tables)
    return solved[:, None, None]


def solution(mesh):
    return jax.shard_map(
        body,
        mesh=mesh,
        in_specs=(
            P(None, "grid", "proc", None, None),
            P(None, "grid", "proc", None),
            P(None, "grid", "proc", None, None, None),
            P(None, "grid", "proc", None, None),
        ),
        out_specs=P(None, "grid", "proc", None, None),
        check_vma=False,
    )
```

profile of v0, /device:TPU:0, one launch (start us, length us, event | category | flops | bytes accessed | tf_op | source)
XLA Modules:
  0.0 210.4 jit_solution(1006689002601257720)
XLA Ops:
  6.5 0.0 copy-start.1
  6.5 0.0 all-gather.5.cloned.1.call-start
  6.5 3.5 %fusion.39 = (bf16[256,1024]{1,0:T(8,128)(2,1)}, f32[256,1024]{1,0:T(8,128)}) fusion(f32[3,1,1,256,1024]{4,3,2,1,0:T(8,128)} %param.4, f32[3,1,1,256,256]{4,3,2,1,0:T(8,128)} %param.7), kind=kOutput, calls=%fused_computation.46 | convolution fusion | flops 805568512 | bytes 2883584 | tf_op jit(solution)/shard_map/dot_general | solution.py:28
  10.1 0.0 all-gather.5.cloned.1.call-update
  10.1 0.0 all-gather.7.cloned.1.call-start
  10.1 0.0 copy-done.1
  10.2 2.5 %fusion.38 = (bf16[1,1,1,16,256,256]{5,4,3,2,1,0:T(8,128)(2,1)S(1)}, bf16[1,1,1,16,256,256]{5,4,3,2,1,0:T(8,128)(2,1)S(1)}) fusion(bf16[2,1,1,16,256,256]{5,4,3,2,1,0:T(8,128)(2,1)} %param.6), kind=kLoop, calls=%fused_computation.45 | loop fusion | bytes 8388608 | tf_op jit(solution)/shard_map/slice | solution.py:57
  12.7 2.6 %convert_bitcast_fusion.1 = bf16[2,8,256,256]{3,1,0,2:T(8,128)(2,1)} fusion(bf16[1,1,1,16,256,256]{5,4,3,2,1,0:T(8,128)(2,1)S(1)} %get-tuple-element.6, s32[16]{0:T(128)S(1)} %get-tuple-element.8), kind=kOutput, calls=%fused_computation.10 | convolution fusion | flops 34603264 | bytes 4194368 | tf_op jit(solution)/shard_map/sq,sij->qij/dot_general | solution.py:21
  15.4 71.0 %all-gather.5.cloned.1.call-done = bf16[2048,1024]{1,0:T(8,128)(2,1)} async-done(((bf16[256,1024]{1,0:T(8,128)(2,1)}), bf16[2048,1024]{1,0:T(8,128)(2,1)}) %all-gather.5.cloned.1.call-update) | async-done | bytes 4194320 | tf_op jit(solution)/shard_map/all_gather | solution.py:43
  86.3 5.5 %fusion.6 = f32[2,256,1024]{2,1,0:T(8,128)S(1)} fusion(bf16[8,256,1024,1]{2,1,0,3:T(8,128)(2,1)} %bitcast.103, bf16[2,8,256,256]{3,1,0,2:T(8,128)(2,1)} %convert_bitcast_fusion.1), kind=kOutput, calls=%fused_computation.11 | convolution fusion | flops 2147483648 | bytes 8388608 | tf_op jit(solution)/shard_map/dkij,kjr->dir/dot_general | solution.py:40
  91.9 0.1 slice_bitcast_fusion.2
  91.9 0.1 collective-permute-start
  92.0 2.6 %collective-permute-done = f32[256,1024]{1,0:T(8,128)S(1)} collective-permute-done((f32[256,1024]{1,0:T(8,128)S(1)}, f32[256,1024]{1,0:T(8,128)S(1)}, u32[]{:S(2)}, u32[]{:S(2)}) %collective-permute-start) | collective-permute-done | bytes 1048608 | tf_op jit(solution)/shard_map/ppermute | solution.py:14
  94.7 3.3 %bitcast_convert_fusion = (bf16[256,1024]{1,0:T(8,128)(2,1)}, f32[1024,256]{0,1:T(8,128)S(1)}) fusion(f32[3,1,1,256,256]{4,3,2,1,0:T(8,128)} %param.7, f32[256,1024]{1,0:T(8,128)S(1)} %collective-permute-done, f32[2,256,1024]{2,1,0:T(8,128)S(1)} %fusion.6, f32[3,1,1,256,1024]{4,3,2,1,0:T(8,128)} %param.4), kind=kOutput, calls=%fused_computation.24 | convolution fusion | flops 806092800 | bytes 4980736 | tf_op jit(solution)/shard_map/dot_general | solution.py:28
  98.0 0.0 all-gather.7.cloned.1.call-update
  98.0 2.6 %convert_bitcast_fusion = bf16[2,8,256,256]{3,1,0,2:T(8,128)(2,1)} fusion(bf16[1,1,1,16,256,256]{5,4,3,2,1,0:T(8,128)(2,1)S(1)} %get-tuple-element.5, s32[16]{0:T(128)S(1)} %get-tuple-element.7), kind=kOutput, calls=%fused_computation.9 | convolution fusion | flops 34603264 | bytes 4194368 | tf_op jit(solution)/shard_map/sq,sij->qij/dot_general | solution.py:21
  100.6 69.2 %all-gather.7.cloned.1.call-done = bf16[2048,1024]{1,0:T(8,128)(2,1)} async-done(((bf16[256,1024]{1,0:T(8,128)(2,1)}), bf16[2048,1024]{1,0:T(8,128)(2,1)}) %all-gather.7.cloned.1.call-update) | async-done | bytes 4194320 | tf_op jit(solution)/shard_map/all_gather | solution.py:43
  169.8 5.5 %fusion.9 = f32[2,256,1024]{2,1,0:T(8,128)S(1)} fusion(bf16[8,256,1024,1]{2,1,0,3:T(8,128)(2,1)} %bitcast.104, bf16[2,8,256,256]{3,1,0,2:T(8,128)(2,1)} %convert_bitcast_fusion), kind=kOutput, calls=%fused_computation.12 | convolution fusion | flops 2147483648 | bytes 8388608 | tf_op jit(solution)/shard_map/dkij,kjr->dir/dot_general | solution.py:40
  175.3 0.1 slice_bitcast_fusion
  175.4 0.0 copy-start
  175.5 1.5 collective-permute-start.1
  177.0 22.2 %collective-permute-done.1 = f32[256,1024]{1,0:T(8,128)S(1)} collective-permute-done((f32[256,1024]{1,0:T(8,128)S(1)}, f32[256,1024]{1,0:T(8,128)S(1)}, u32[]{:S(2)}, u32[]{:S(2)}) %collective-permute-start.1) | collective-permute-done | bytes 1048608 | tf_op jit(solution)/shard_map/ppermute | solution.py:14
  199.2 2.5 %convolution_bitcast_fusion = f32[1,256,1024]{2,1,0:T(8,128)S(1)} fusion(f32[256,1024]{1,0:T(8,128)S(1)} %collective-permute-done.1, f32[2,256,1024]{2,1,0:T(8,128)S(1)} %fusion.9, f32[3,1,1,256,1024]{4,3,2,1,0:T(8,128)} %param.4, f32[3,1,1,256,256]{4,3,2,1,0:T(8,128)} %param.7), kind=kOutput, calls=%fused_computation.13 | convolution fusion | flops 805830656 | bytes 4456448 | tf_op jit(solution)/shard_map/dot_general | solution.py:28
  201.7 0.0 copy-done
  201.7 1.9 maximum_bitcast_fusion
  (1 shorter events, 0.0 us)
Async XLA Ops:
  6.5 3.6 %copy-start.1 = (s32[2,1,1,16]{3,2,1,0:T(1,128)S(1)}, s32[2,1,1,16]{3,2,1,0:T(1,128)}, u32[]{:S(2)}) copy-start(s32[2,1,1,16]{3,2,1,0:T(1,128)} %param.5) | copy-start | bytes 388
  6.5 79.8 %all-gather.5.cloned.1.call-start = ((), (), s32[]{:S(2)}) async-start(), calls=%async_computation | async-start | bytes 4718592 | tf_op jit(solution)/shard_map/all_gather | solution.py:43
  10.1 159.7 %all-gather.7.cloned.1.call-start = ((), (), s32[]{:S(2)}) async-start(), calls=%async_computation.1 | async-start | bytes 4718592 | tf_op jit(solution)/shard_map/all_gather | solution.py:43
  91.9 2.7 %collective-permute-start = (f32[256,1024]{1,0:T(8,128)S(1)}, f32[256,1024]{1,0:T(8,128)S(1)}, u32[]{:S(2)}, u32[]{:S(2)}) collective-permute-start(f32[256,1024]{1,0:T(8,128)S(1)} %slice_bitcast_fusion.2), channel_id=1, source_target_pairs={{0,8},{8,0},{16,24},{24,16},{1,9},{9,1},{17,25},{25,17},{2,10},{10... | collective-permute-start | bytes 3145736 | tf_op jit(solution)/shard_map/ppermute | solution.py:14
  175.4 26.3 %copy-start = (f32[256,1024]{1,0:T(8,128)S(1)}, f32[256,1024]{1,0:T(8,128)}, u32[]{:S(2)}) copy-start(f32[256,1024]{1,0:T(8,128)} %get-tuple-element.10) | copy-start | bytes 3145732
  175.5 23.8 %collective-permute-start.1 = (f32[256,1024]{1,0:T(8,128)S(1)}, f32[256,1024]{1,0:T(8,128)S(1)}, u32[]{:S(2)}, u32[]{:S(2)}) collective-permute-start(f32[256,1024]{1,0:T(8,128)S(1)} %slice_bitcast_fusion), channel_id=1, source_target_pairs={{0,16},{16,0},{8,24},{24,8},{1,17},{17,1},{9,25},{25,9},{2,18},{18... | collective-permute-start | bytes 3145736 | tf_op jit(solution)/shard_map/ppermute | solution.py:14
Sparse Core Ops, SparseCore 0:
  10.2 76.0 all-gather.4
  98.1 71.6 all-gather.6
where the time goes:
time: 211 us; the launch traced here: 210 us
  waiting for transfers between devices  165 us (78%)
  matrix products  25.6 us (12%)
  between operations  13.5 us (6%)
  local copies, waits for them, and re-layouts  2.72 us (1%)
    all_gather x2, waiting for transfers between devices, solve_levels(): lax.all_gather(outgoing, 'proc', axis=0, tiled=True)  140 us
    ppermute x2, waiting for transfers between devices, from_partner(): return lax.ppermute(block, axis, route)  24.9 us
    dot_general x2, matrix products, solve_levels(): jnp.einsum('dkij,kjr->dir', dense_table, lax.all_gather(outgoing, 'proc',...  11 us
    dot_general x3, matrix products, diagonal_solve(): jnp.dot(factor, values, precision=lax.Precision.HIGHEST, preferred_elemen...  9.32 us
    dot_general x2, matrix products, build_table(): jnp.einsum('sq,sij->qij', onehot, tile_set, preferred_element_type=jnp.fl...  5.28 us
  transfers between devices with their start and end apart: 4, of which 4 were waited for; matrix products, arithmetic and copies ran while one was open for 4% of the time, Pallas kernels for 0%

commit v1 on v0

v1 whole, which is shorter than its diff:
```python
import functools

import jax
import jax.numpy as jnp
from jax import lax
from jax.experimental import pallas as pl
from jax.experimental.pallas import tpu as pltpu
from jax.sharding import PartitionSpec as P

MESH = pl.DeviceIdType.MESH
CHUNKS = 4


def flip(index, bit):
    return index + bit * (1 - 2 * lax.rem(lax.div(index, bit), 2))


def kernel(procs, chunks, rhs_hbm, pairs, tiles_hbm, dinv_hbm, out_hbm,
           rhs_v, tiles_v, dinv_v, out_v, table, held, near, away, come,
           in_sem, out_sem, send_sem, recv_sem, away_sem, come_sem):
    levels, rows, columns = rhs_v.shape
    trans, slots = tiles_v.shape[:2]
    width = columns // chunks
    half = rows // 2
    depth = procs // 2
    grid = lax.axis_index("grid")
    me = lax.axis_index("proc")
    y, z = lax.rem(me, 2), lax.div(me, 2)
    across = me + 1 - 2 * y
    twin_z = flip(z, 1)
    twin = twin_z * 2 + y
    partners = [flip(grid, 1 << t) for t in range(trans)]

    loads = []
    for level in range(levels):
        loads.append((
            pltpu.make_async_copy(dinv_hbm.at[level], dinv_v.at[level], in_sem.at[level, 0]),
            pltpu.make_async_copy(rhs_hbm.at[level], rhs_v.at[level], in_sem.at[level, 1]),
        ))
    tile_loads = [
        pltpu.make_async_copy(tiles_hbm.at[t], tiles_v.at[t], in_sem.at[t, 2]) for t in range(trans)
    ]
    for copy in loads[0]:
        copy.start()

    barrier = pltpu.get_barrier_semaphore()

    def greet(device):
        pl.semaphore_signal(barrier, inc=1, device_id=device, device_id_type=MESH)

    greet({"proc": across})
    for partner in partners:
        greet({"grid": partner})
    pl.when(z > 0)(lambda: greet({"proc": me - 2}))
    pl.when(z < depth - 1)(lambda: greet({"proc": me + 2}))

    for copy in tile_loads[:1] + list(loads[1]) + tile_loads[1:]:
        copy.start()
    for level in range(2, levels):
        for copy in loads[level]:
            copy.start()

    def cols(c):
        return pl.ds(pl.multiple_of(c * width, width), width)

    def send(t, c, block, way, target, part=None):
        src = held.at[t, c, block]
        slot = 0
        if part is not None:
            src = held.at[t, c, block, pl.ds(part * half, half)]
            slot = part
        return pltpu.make_async_remote_copy(
            src_ref=src, dst_ref=src,
            send_sem=send_sem.at[t, c, block, way],
            recv_sem=recv_sem.at[t, c, block, slot],
            device_id={"proc": target}, device_id_type=MESH,
        )

    def arrive(t, c, block, part=None):
        send(t, c, block, 0, across, part).wait_recv()

    def own(t, c, act):
        act(send(t, c, me, 2, across))
        pl.when(z > 0)(lambda: act(send(t, c, me, 0, me - 2)))
        pl.when(z < depth - 1)(lambda: act(send(t, c, me, 1, me + 2)))

    def relay(t, c, act, wait):
        for d in range(1, depth):
            for side in (1, -1):
                block = me + 2 * d * side

                def there(block=block, d=d, side=side):
                    if wait:
                        arrive(t, c, block)
                    if side == 1:
                        pl.when(z > 0)(lambda: act(send(t, c, block, 0, me - 2)))
                    else:
                        pl.when(z < depth - 1)(lambda: act(send(t, c, block, 1, me + 2)))
                    if d == 1:
                        mine = block == twin
                        pl.when(mine)(lambda: act(send(t, c, block, 2, across, 1)))
                        pl.when(jnp.logical_not(mine))(lambda: act(send(t, c, block, 2, across)))
                    else:
                        act(send(t, c, block, 2, across))

                pl.when((z + d < depth) if side == 1 else (z >= d))(there)
            if d == 1:
                if wait:
                    arrive(t, c, across)
                act(send(t, c, across, 0, twin, 0))

    def settle(t, c):
        for d in range(1, depth):
            for side in (1, -1):
                block = across + 2 * d * side

                def there(block=block, d=d):
                    if d == 1:
                        mine = lax.div(block, 2) == twin_z

                        @pl.when(mine)
                        def _():
                            arrive(t, c, block, 0)
                            arrive(t, c, block, 1)

                        pl.when(jnp.logical_not(mine))(lambda: arrive(t, c, block))
                    else:
                        arrive(t, c, block)

                pl.when((z + d < depth) if side == 1 else (z >= d))(there)

    def keep(level, c, value):
        out_v[level, :, cols(c)] = value
        store(level, c).start()

    def store(level, c):
        return pltpu.make_async_copy(
            out_v.at[level, :, cols(c)], out_hbm.at[level, :, cols(c)], out_sem.at[level, c]
        )

    def solve(level, c, values):
        return jnp.dot(dinv_v[level], values, precision=lax.Precision.HIGHEST,
                       preferred_element_type=jnp.float32)

    def first(c):
        value = solve(0, c, rhs_v[0, :, cols(c)])
        keep(0, c, value)
        held[0, c, me] = value.astype(held.dtype)

    def exchange(t, c):
        return pltpu.make_async_remote_copy(
            src_ref=away.at[t, c], dst_ref=come.at[t, c],
            send_sem=away_sem.at[t, c], recv_sem=come_sem.at[t, c],
            device_id={"grid": partners[t]}, device_id_type=MESH,
        )

    def multiply(t, c):
        blocks = held[t, c].reshape(procs * rows, width)
        away[t, c] = jnp.dot(table[t, 1], blocks, preferred_element_type=jnp.float32)
        exchange(t, c).start()
        near[t, c] = jnp.dot(table[t, 0], blocks, preferred_element_type=jnp.float32)

    def update(t, c):
        exchange(t, c).wait_recv()
        total = near[t, c] + come[t, c]
        value = solve(t + 1, c, rhs_v[t + 1, :, cols(c)] - total)
        keep(t + 1, c, value)
        if t + 1 < trans:
            held[t + 1, c, me] = value.astype(held.dtype)
            own(t + 1, c, lambda copy: copy.start())

    def build(t):
        for copy in (tile_loads if t == 0 else []) + list(loads[t + 1]):
            copy.wait()
        for d in range(2):
            def fill(k, _, d=d):
                slot = jnp.int32(0)
                found = jnp.int32(0)
                for s in range(slots):
                    hit = pairs[t, s] == d * procs + k
                    slot = jnp.where(hit, s, slot)
                    found = jnp.where(hit, 1, found)
                tile = tiles_v[t, slot].astype(jnp.float32) * found.astype(jnp.float32)
                table[t, d, :, pl.ds(pl.multiple_of(k * rows, rows), rows)] = tile.astype(table.dtype)
                return 0
            lax.fori_loop(0, procs, fill, 0)

    def each(lower, upper, step):
        def run(c, _):
            step(c)
            return 0
        lax.fori_loop(lower, upper, run, 0)

    for copy in loads[0]:
        copy.wait()
    first(0)
    pl.semaphore_wait(
        barrier,
        1 + trans + (z > 0).astype(jnp.int32) + (z < depth - 1).astype(jnp.int32),
    )
    own(0, 0, lambda copy: copy.start())

    @functools.partial(each, 1, chunks)
    def _(c):
        first(c)
        own(0, c, lambda copy: copy.start())

    build(0)
    for t in range(trans):
        relay(t, 0, lambda copy: copy.start(), True)
        if t > 0:
            update(t - 1, chunks - 1)
        settle(t, 0)
        multiply(t, 0)
        if t + 1 < trans:
            build(t + 1)

        @functools.partial(each, 1, chunks)
        def _(c):
            relay(t, c, lambda copy: copy.start(), True)
            update(t, c - 1)
            settle(t, c)
            multiply(t, c)

    update(trans - 1, chunks - 1)

    @functools.partial(each, 0, chunks)
    def _(c):
        for t in range(trans):
            own(t, c, lambda copy: copy.wait_send())
            relay(t, c, lambda copy: copy.wait_send(), False)
            exchange(t, c).wait_send()
        for level in range(levels):
            store(level, c).wait()


def body(rhs, tile_pairs, tiles, dinv):
    rhs_block, pairs = rhs[:, 0, 0], tile_pairs[:, 0, 0]
    tile_block, dinv_block = tiles[:, 0, 0], dinv[:, 0, 0]
    procs = lax.axis_size("proc")
    levels, rows, columns = rhs_block.shape
    trans, slots = pairs.shape
    chunks = CHUNKS
    width = columns // chunks
    any_spec = pl.BlockSpec(memory_space=pl.ANY)
    flops = 2 * rows * rows * columns * (levels * 6 + trans * 2 * procs)
    solved = pl.pallas_call(
        functools.partial(kernel, procs, chunks),
        out_shape=jax.ShapeDtypeStruct(rhs_block.shape, jnp.float32),
        in_specs=[any_spec, pl.BlockSpec(memory_space=pltpu.SMEM), any_spec, any_spec],
        out_specs=any_spec,
        scratch_shapes=[
            pltpu.VMEM((levels, rows, columns), jnp.float32),
            pltpu.VMEM((trans, slots, rows, rows), jnp.bfloat16),
            pltpu.VMEM((levels, rows, rows), jnp.float32),
            pltpu.VMEM((levels, rows, columns), jnp.float32),
            pltpu.VMEM((trans, 2, rows, procs * rows), jnp.bfloat16),
            pltpu.VMEM((trans, chunks, procs, rows, width), jnp.bfloat16),
            pltpu.VMEM((trans, chunks, rows, width), jnp.float32),
            pltpu.VMEM((trans, chunks, rows, width), jnp.float32),
            pltpu.VMEM((trans, chunks, rows, width), jnp.float32),
            pltpu.SemaphoreType.DMA((levels, 3)),
            pltpu.SemaphoreType.DMA((levels, chunks)),
            pltpu.SemaphoreType.DMA((trans, chunks, procs, 3)),
            pltpu.SemaphoreType.DMA((trans, chunks, procs, 2)),
            pltpu.SemaphoreType.DMA((trans, chunks)),
            pltpu.SemaphoreType.DMA((trans, chunks)),
        ],
        compiler_params=pltpu.CompilerParams(
            collective_id=0, has_side_effects=True, vmem_limit_bytes=60 * 1024 * 1024
        ),
        cost_estimate=pl.CostEstimate(
            flops=flops, bytes_accessed=14 * 1024 * 1024, transcendentals=0
        ),
    )(rhs_block, pairs, tile_block, dinv_block)
    return solved[:, None, None]


def solution(mesh):
    return jax.shard_map(
        body,
        mesh=mesh,
        in_specs=(
            P(None, "grid", "proc", None, None),
            P(None, "grid", "proc", None),
            P(None, "grid", "proc", None, None, None),
            P(None, "grid", "proc", None, None),
        ),
        out_specs=P(None, "grid", "proc", None, None),
        check_vma=False,
    )
```

time: 211 us -> 120 us (0.57)
  waiting for transfers between devices: 165 us -> 0 us
  Pallas kernels: 0 us -> 116 us
  matrix products: 25.6 us -> 0 us
  between operations: 13.5 us -> 0.01 us
    all_gather x2 -> x0, waiting for transfers between devices: 140 us -> none  [solve_levels(): lax.all_gather(outgoing, 'proc', axis=0, tiled=True)]
    pallas_call x0 -> x1, Pallas kernels: none -> 116 us  [body(): pl.pallas_call(functools.partial(kernel, procs, chunks), out_shape=jax.Sh...]
    dot_general x7 -> x0, matrix products: 25.6 us -> none  [the longest x2 11 us: solve_levels(): jnp.einsum('dkij,kjr->dir', dense_table, lax.all_gather(outgoing, 'proc',...]
    ppermute x2 -> x0, waiting for transfers between devices: 24.9 us -> none  [from_partner(): return lax.ppermute(block, axis, route)]
    unnamed x4 -> x1, local copies, waits for them, and re-layouts: 0.01 us -> 3.97 us
    slice x1 -> x0, local copies, waits for them, and re-layouts: 2.54 us -> none  [body(): tiles[number, 0, 0]]
  transfers between devices with their start and end apart: 4 -> 0, of which waited for: 4 -> 0; matrix products, arithmetic and copies ran while one was open for 4% -> 0% of each run, Pallas kernels for 0% -> 0%
where the time goes in v1:
time: 120 us
  Pallas kernels  116 us (97%)
  local copies, waits for them, and re-layouts  3.97 us (3%)
    pallas_call x1, Pallas kernels, body(): pl.pallas_call(functools.partial(kernel, procs, chunks), out_shape=jax.Sh...  116 us
    unnamed x1, local copies, waits for them, and re-layouts  3.97 us

profile of v1, /device:TPU:0, one launch (start us, length us, event | category | flops | bytes accessed | tf_op | source)
XLA Modules:
  0.0 119.7 jit_solution(7818070230649123438)
XLA Ops:
  0.0 115.7 %shard_map.46 = f32[3,256,1024]{2,1,0:T(8,128)} custom-call(f32[3,256,1024]{2,1,0:T(8,128)} %bitcast.9, s32[2,16]{1,0:T(2,128)} %bitcast.11, bf16[2,16,256,256]{3,2,1,0:T(8,128)(2,1)} %bitcast.8, f32[3,256,256]{2,1,0:T(8,128)} %bitcast.10), custom_call_target="tpu_custom_call" | custom-call | flops 6710886400 | bytes 14680064 | tf_op jit(solution)/shard_map/pallas_call | solution.py:247
  115.7 4.0 %copy.7 = f32[3,1,1,256,1024]{4,3,2,1,0:T(8,128)} copy(f32[3,1,1,256,1024]{4,3,2,1,0:T(8,128)} %bitcast.7) | data formatting | bytes 6291456

commit v2 on v1

--- a/solution.py
+++ b/solution.py
@@ -9,6 +9,7 @@
 
 MESH = pl.DeviceIdType.MESH
 CHUNKS = 4
+LEAD = 2
 
 
 def flip(index, bit):
@@ -84,30 +85,29 @@
         pl.when(z > 0)(lambda: act(send(t, c, me, 0, me - 2)))
         pl.when(z < depth - 1)(lambda: act(send(t, c, me, 1, me + 2)))
 
-    def relay(t, c, act, wait):
-        for d in range(1, depth):
-            for side in (1, -1):
-                block = me + 2 * d * side
-
-                def there(block=block, d=d, side=side):
-                    if wait:
-                        arrive(t, c, block)
-                    if side == 1:
-                        pl.when(z > 0)(lambda: act(send(t, c, block, 0, me - 2)))
-                    else:
-                        pl.when(z < depth - 1)(lambda: act(send(t, c, block, 1, me + 2)))
-                    if d == 1:
-                        mine = block == twin
-                        pl.when(mine)(lambda: act(send(t, c, block, 2, across, 1)))
-                        pl.when(jnp.logical_not(mine))(lambda: act(send(t, c, block, 2, across)))
-                    else:
-                        act(send(t, c, block, 2, across))
-
-                pl.when((z + d < depth) if side == 1 else (z >= d))(there)
-            if d == 1:
+    def hop(t, c, d, act, wait):
+        for side in (1, -1):
+            block = me + 2 * d * side
+
+            def there(block=block, side=side):
                 if wait:
-                    arrive(t, c, across)
-                act(send(t, c, across, 0, twin, 0))
+                    arrive(t, c, block)
+                if side == 1:
+                    pl.when(z > 0)(lambda: act(send(t, c, block, 0, me - 2)))
+                else:
+                    pl.when(z < depth - 1)(lambda: act(send(t, c, block, 1, me + 2)))
+                if d == 1:
+                    mine = block == twin
+                    pl.when(mine)(lambda: act(send(t, c, block, 2, across, 1)))
+                    pl.when(jnp.logical_not(mine))(lambda: act(send(t, c, block, 2, across)))
+                else:
+                    act(send(t, c, block, 2, across))
+
+            pl.when((z + d < depth) if side == 1 else (z >= d))(there)
+        if d == 1:
+            if wait:
+                arrive(t, c, across)
+            act(send(t, c, across, 0, twin, 0))
 
     def settle(t, c):
         for d in range(1, depth):
@@ -199,36 +199,50 @@
         1 + trans + (z > 0).astype(jnp.int32) + (z < depth - 1).astype(jnp.int32),
     )
     own(0, 0, lambda copy: copy.start())
-
-    @functools.partial(each, 1, chunks)
+    lead = min(LEAD, chunks)
+
+    @functools.partial(each, 1, lead)
     def _(c):
         first(c)
         own(0, c, lambda copy: copy.start())
 
     build(0)
-    for t in range(trans):
-        relay(t, 0, lambda copy: copy.start(), True)
-        if t > 0:
-            update(t - 1, chunks - 1)
-        settle(t, 0)
-        multiply(t, 0)
-        if t + 1 < trans:
-            build(t + 1)
-
-        @functools.partial(each, 1, chunks)
-        def _(c):
-            relay(t, c, lambda copy: copy.start(), True)
-            update(t, c - 1)
+    stride = max(chunks, depth + 2)
+
+    @functools.partial(each, 0, (trans - 1) * stride + chunks + depth)
+    def _(tick):
+        def at(lag, step):
+            for t in range(trans):
+                c = tick - lag - t * stride
+                pl.when(jnp.logical_and(c >= 0, c < chunks))(functools.partial(step, t, c))
+
+        for d in range(depth - 1, 0, -1):
+            for t in range(trans):
+                c = tick - (d - 1) - t * stride
+                pl.when(jnp.logical_and(c >= 0, c < chunks))(
+                    functools.partial(hop, t, c, d, lambda copy: copy.start(), True))
+
+        @pl.when(tick + lead < chunks)
+        def _():
+            first(tick + lead)
+            own(0, tick + lead, lambda copy: copy.start())
+
+        at(depth, update)
+
+        def gathered(t, c):
             settle(t, c)
             multiply(t, c)
 
-    update(trans - 1, chunks - 1)
+        at(depth - 1, gathered)
+        for t in range(1, trans):
+            pl.when(tick == t * stride)(functools.partial(build, t))
 
     @functools.partial(each, 0, chunks)
     def _(c):
         for t in range(trans):
             own(t, c, lambda copy: copy.wait_send())
-            relay(t, c, lambda copy: copy.wait_send(), False)
+            for d in range(1, depth):
+                hop(t, c, d, lambda copy: copy.wait_send(), False)
             exchange(t, c).wait_send()
         for level in range(levels):
             store(level, c).wait()

time: 120 us -> 112 us (0.933)
  Pallas kernels: 116 us -> 108 us
    pallas_call x1, Pallas kernels: 116 us -> 108 us  [body(): pl.pallas_call(functools.partial(kernel, procs, chunks), out_shape=jax.Sh...]
where the time goes in v2:
time: 112 us
  Pallas kernels  108 us (96%)
  local copies, waits for them, and re-layouts  3.97 us (4%)
    pallas_call x1, Pallas kernels, body(): pl.pallas_call(functools.partial(kernel, procs, chunks), out_shape=jax.Sh...  108 us
    unnamed x1, local copies, waits for them, and re-layouts  3.97 us

profile of v2, /device:TPU:0, one launch (start us, length us, event | category | flops | bytes accessed | tf_op | source)
XLA Modules:
  0.0 111.5 jit_solution(12596775633130964255)
XLA Ops:
  0.0 107.6 %shard_map.46 = f32[3,256,1024]{2,1,0:T(8,128)} custom-call(f32[3,256,1024]{2,1,0:T(8,128)} %bitcast.9, s32[2,16]{1,0:T(2,128)} %bitcast.11, bf16[2,16,256,256]{3,2,1,0:T(8,128)(2,1)} %bitcast.8, f32[3,256,256]{2,1,0:T(8,128)} %bitcast.10), custom_call_target="tpu_custom_call" | custom-call | flops 6710886400 | bytes 14680064 | tf_op jit(solution)/shard_map/pallas_call | solution.py:261
  107.6 4.0 %copy.7 = f32[3,1,1,256,1024]{4,3,2,1,0:T(8,128)} copy(f32[3,1,1,256,1024]{4,3,2,1,0:T(8,128)} %bitcast.7) | data formatting | bytes 6291456

commit v3 on v2

--- a/solution.py
+++ b/solution.py
@@ -8,8 +8,8 @@
 from jax.sharding import PartitionSpec as P
 
 MESH = pl.DeviceIdType.MESH
-CHUNKS = 4
-LEAD = 2
+CHUNKS = 8
+LEAD = 3
 
 
 def flip(index, bit):

time: 112 us -> 118 us (1.054)
  Pallas kernels: 108 us -> 114 us
    pallas_call x1, Pallas kernels: 108 us -> 114 us  [body(): pl.pallas_call(functools.partial(kernel, procs, chunks), out_shape=jax.Sh...]
where the time goes in v3:
time: 118 us
  Pallas kernels  114 us (97%)
  local copies, waits for them, and re-layouts  3.97 us (3%)
    pallas_call x1, Pallas kernels, body(): pl.pallas_call(functools.partial(kernel, procs, chunks), out_shape=jax.Sh...  114 us
    unnamed x1, local copies, waits for them, and re-layouts  3.97 us

profile of v3, /device:TPU:0, one launch (start us, length us, event | category | flops | bytes accessed | tf_op | source)
XLA Modules:
  0.0 118.0 jit_solution(3777516346426976516)
XLA Ops:
  0.0 114.0 %shard_map.46 = f32[3,256,1024]{2,1,0:T(8,128)} custom-call(f32[3,256,1024]{2,1,0:T(8,128)} %bitcast.9, s32[2,16]{1,0:T(2,128)} %bitcast.11, bf16[2,16,256,256]{3,2,1,0:T(8,128)(2,1)} %bitcast.8, f32[3,256,256]{2,1,0:T(8,128)} %bitcast.10), custom_call_target="tpu_custom_call" | custom-call | flops 6710886400 | bytes 14680064 | tf_op jit(solution)/shard_map/pallas_call | solution.py:261
  114.0 4.0 %copy.7 = f32[3,1,1,256,1024]{4,3,2,1,0:T(8,128)} copy(f32[3,1,1,256,1024]{4,3,2,1,0:T(8,128)} %bitcast.7) | data formatting | bytes 6291456

commit v4 on v2

--- a/solution.py
+++ b/solution.py
@@ -9,7 +9,7 @@
 
 MESH = pl.DeviceIdType.MESH
 CHUNKS = 4
-LEAD = 2
+LEAD = 4
 
 
 def flip(index, bit):
@@ -206,8 +206,9 @@
         first(c)
         own(0, c, lambda copy: copy.start())
 
-    build(0)
-    stride = max(chunks, depth + 2)
+    for t in range(trans):
+        build(t)
+    stride = max(chunks, depth + 1)
 
     @functools.partial(each, 0, (trans - 1) * stride + chunks + depth)
     def _(tick):
@@ -234,8 +235,6 @@
             multiply(t, c)
 
         at(depth - 1, gathered)
-        for t in range(1, trans):
-            pl.when(tick == t * stride)(functools.partial(build, t))
 
     @functools.partial(each, 0, chunks)
     def _(c):

time: 112 us -> 114 us (1.018)
  Pallas kernels: 108 us -> 110 us
    pallas_call x1, Pallas kernels: 108 us -> 110 us  [body(): pl.pallas_call(functools.partial(kernel, procs, chunks), out_shape=jax.Sh...]
where the time goes in v4:
time: 114 us
  Pallas kernels  110 us (96%)
  local copies, waits for them, and re-layouts  3.97 us (3%)
    pallas_call x1, Pallas kernels, body(): pl.pallas_call(functools.partial(kernel, procs, chunks), out_shape=jax.Sh...  110 us
    unnamed x1, local copies, waits for them, and re-layouts  3.97 us

profile of v4, /device:TPU:0, one launch (start us, length us, event | category | flops | bytes accessed | tf_op | source)
XLA Modules:
  0.0 114.1 jit_solution(6988506492828952020)
XLA Ops:
  0.0 110.1 %shard_map.46 = f32[3,256,1024]{2,1,0:T(8,128)} custom-call(f32[3,256,1024]{2,1,0:T(8,128)} %bitcast.9, s32[2,16]{1,0:T(2,128)} %bitcast.11, bf16[2,16,256,256]{3,2,1,0:T(8,128)(2,1)} %bitcast.8, f32[3,256,256]{2,1,0:T(8,128)} %bitcast.10), custom_call_target="tpu_custom_call" | custom-call | flops 6710886400 | bytes 14680064 | tf_op jit(solution)/shard_map/pallas_call | solution.py:260
  110.1 4.0 %copy.7 = f32[3,1,1,256,1024]{4,3,2,1,0:T(8,128)} copy(f32[3,1,1,256,1024]{4,3,2,1,0:T(8,128)} %bitcast.7) | data formatting | bytes 6291456
